TPU v7x, 128 devices: a whole 4x4x4 slice. The times are simulated.
128 devices in a mesh: leaf: 4 (over y), row: 8 (over z, core), col: 4 (over x).
Axes of the slice: x: 4, y: 4, z: 4, core: 2. Of those that a mesh axis runs over, the one named last changes fastest.
Arguments:
- leaf_rhs: float32 [4, 8, 4, 1, 128, 256], P('leaf', 'row', 'col'), may hold values from -6 to 6
- mid_rhs: float32 [4, 8, 4, 1, 128, 256], P('leaf', 'row', 'col'), may hold values from -6 to 6
- top_rhs: float32 [4, 8, 4, 1, 128, 256], P('leaf', 'row', 'col'), may hold values from -6 to 6
- leaf_inverse: bfloat16 [4, 8, 4, 128, 4, 8, 128], P('leaf', 'row', None, None, 'col'), as said below
- mid_inverse: bfloat16 [4, 8, 4, 128, 4, 16, 128], P('leaf', 'row', None, None, 'col'), as said below
- top_inverse: bfloat16 [4, 8, 4, 128, 4, 32, 128], P('leaf', 'row', None, None, 'col'), as said below
- leaf_coupling: bfloat16 [4, 8, 4, 6, 128, 4, 8, 128], P('leaf', 'row', None, None, None, 'col'), may hold values from -0.09375 to 0.09375
- mid_coupling: bfloat16 [4, 8, 2, 4, 128, 4, 16, 128], P('leaf', 'row', None, None, None, 'col'), may hold values from -0.0625 to 0.0625
- leaf_targets: int32 [4, 8, 4, 6], P('leaf', 'row'), may hold values from 0 to 7, as said below
- leaf_counts: int32 [4, 8, 4], P('leaf', 'row'), may hold values from 1 to 6, as said below
- mid_targets: int32 [4, 8, 2, 4], P('leaf', 'row'), may hold values from 0 to 3, as said below
- mid_counts: int32 [4, 8, 2], P('leaf', 'row'), may hold values from 1 to 4, as said below
Outputs:
- leaf_solution: float32 [4, 8, 4, 1, 128, 256], P('leaf', 'row', 'col')
- mid_solution: float32 [4, 8, 4, 1, 128, 256], P('leaf', 'row', 'col')
- top_solution: float32 [4, 8, 4, 1, 128, 256], P('leaf', 'row', 'col')
Inputs may be any that keep to these rules, and one draw needn't show every extreme that they name: `leaf_inverse`: every inverse is zero above its diagonal. `mid_inverse`: zero above the diagonal. `top_inverse`: zero above the diagonal. `leaf_targets`: live slots of one owner row and source are distinct and name a middle tile only when that middle separator is the source's ancestor (i div 2 == k div 2). `leaf_counts`: never more than the owner row's allowed targets for that source; 6 is reached in every draw. `mid_targets`: live slots of one owner row and source are distinct. `mid_counts`: 4 is reached in every draw.
All inputs are finite; a program needn't handle non-finite values.
Results may differ from a plain program's by a relative error of at most 0.034.
Values may be sent and summed in bfloat16 or wider, within the bound.
A program may use at most 128 MiB of HBM per device.

v0:
```python
import jax
import jax.numpy as jnp
from jax import lax
from jax.sharding import PartitionSpec as P

precise = lax.Precision.HIGHEST


def shards(
    leaf_rhs,
    mid_rhs,
    top_rhs,
    leaf_inverse,
    mid_inverse,
    top_inverse,
    leaf_coupling,
    mid_coupling,
    leaf_targets,
    leaf_counts,
    mid_targets,
    mid_counts,
):
    leaf_count = lax.axis_size("leaf")
    row_count = lax.axis_size("row")
    col_count = lax.axis_size("col")
    tile_depth = leaf_rhs.shape[3]
    tile_rows = leaf_rhs.shape[4]
    rhs_width = leaf_rhs.shape[5]
    leaf_index = lax.axis_index("leaf")

    def gather_all(vector):
        return lax.all_gather(vector, ("leaf", "row"), axis=0, tiled=True)

    def own_group(gathered, span_leaves):
        length = span_leaves * row_count * tile_depth
        return lax.dynamic_slice_in_dim(gathered, leaf_index // span_leaves * length, length, 0)

    def column_sum(stacked):
        return lax.psum_scatter(
            stacked.astype(jnp.bfloat16), "col", scatter_dimension=1, tiled=True
        ).astype(jnp.float32)

    def row_tiles(vector):
        return lax.all_gather(vector, "col", axis=0, tiled=True)

    def group_sum(partial_value):
        return lax.psum_scatter(
            partial_value.astype(jnp.bfloat16), ("leaf", "row"), scatter_dimension=0, tiled=True
        ).astype(jnp.float32)

    def forward_solve(inverse, inputs):
        matrix = inverse.reshape(col_count * tile_depth * tile_rows, -1)
        product = jnp.dot(matrix, inputs.reshape(-1, rhs_width), preferred_element_type=jnp.float32)
        return column_sum(product.reshape(1, col_count, tile_depth, tile_rows, rhs_width))[0, 0]

    def backward_product(inverse, vector):
        matrix = inverse.reshape(col_count * tile_depth * tile_rows, -1)
        values = row_tiles(vector).reshape(-1, rhs_width)
        product = jnp.einsum("rc,rn->cn", matrix, values, preferred_element_type=jnp.float32)
        return product.reshape(-1, tile_rows, rhs_width)

    def backward_solve(inverse, vector, span_leaves):
        partial_value = backward_product(inverse, vector)
        padded = jnp.zeros((leaf_count * row_count * tile_depth, tile_rows, rhs_width), jnp.float32)
        offset = leaf_index // span_leaves * span_leaves * row_count * tile_depth
        return group_sum(lax.dynamic_update_slice_in_dim(padded, partial_value, offset, 0))

    def live_slots(targets, counts):
        return jnp.arange(targets.shape[1], dtype=jnp.int32)[None, :] < counts[:, None]

    def couple_forward(coupling, targets, counts, solved, local_tiles):
        sources, slot_count = targets.shape
        matrix = coupling.reshape(sources, slot_count * tile_rows, -1)
        inputs = solved.reshape(sources, -1, rhs_width)
        partial_value = jnp.einsum(
            "ksc,kcn->ksn", matrix, inputs, preferred_element_type=jnp.float32
        )
        partial_value = partial_value.reshape(sources, slot_count, tile_rows * rhs_width)
        matches = targets[None] == jnp.arange(local_tiles, dtype=jnp.int32)[:, None, None]
        select = (matches & live_slots(targets, counts)[None]).astype(jnp.float32)
        buffer = jnp.einsum("vki,kim->vm", select, partial_value, precision=precise)
        return buffer.reshape(-1, col_count, tile_depth, tile_rows, rhs_width)

    def couple_backward(coupling, targets, counts, ancestors):
        sources, slot_count = targets.shape
        matrix = coupling.reshape(sources, slot_count * tile_rows, -1)
        live = live_slots(targets, counts).astype(jnp.bfloat16)
        chosen = jnp.take(ancestors, targets, axis=0) * live[:, :, None, None]
        contrib = jnp.einsum(
            "ksc,ksn->kcn",
            matrix,
            chosen.reshape(sources, slot_count * tile_rows, rhs_width),
            preferred_element_type=jnp.float32,
        )
        return group_sum(contrib.reshape(-1, tile_rows, rhs_width))

    leaf_slab = leaf_coupling[0, 0, :, :, :, 0]
    mid_slab = mid_coupling[0, 0, :, :, :, 0]
    leaf_input = leaf_rhs[0, 0, 0].astype(jnp.bfloat16)
    leaf_columns = own_group(gather_all(leaf_input), 1)
    leaf_forward = forward_solve(leaf_inverse, leaf_columns)
    leaf_solved = gather_all(leaf_forward.astype(jnp.bfloat16))
    leaf_buffer = couple_forward(
        leaf_slab, leaf_targets[0, 0], leaf_counts[0, 0], leaf_solved, 2 * col_count * tile_depth
    )
    both_parts = column_sum(leaf_buffer)
    mid_update = both_parts[0, 0]
    top_early = both_parts[1, 0]
    mid_input = (mid_rhs[0, 0, 0] - mid_update).astype(jnp.bfloat16)
    mid_columns = own_group(gather_all(mid_input), 2)
    mid_forward = forward_solve(mid_inverse, mid_columns)
    mid_solved = gather_all(mid_forward.astype(jnp.bfloat16))
    mid_buffer = couple_forward(
        mid_slab, mid_targets[0, 0], mid_counts[0, 0], mid_solved, col_count * tile_depth
    )
    top_input = (top_rhs[0, 0, 0] - top_early - column_sum(mid_buffer)[0, 0]).astype(jnp.bfloat16)
    top_forward = forward_solve(top_inverse, gather_all(top_input))
    top_solution = backward_solve(top_inverse, top_forward.astype(jnp.bfloat16), leaf_count)
    top_local = row_tiles(top_solution.astype(jnp.bfloat16))
    mid_return = couple_backward(mid_slab, mid_targets[0, 0], mid_counts[0, 0], top_local)
    mid_back_in = (mid_forward - mid_return).astype(jnp.bfloat16)
    mid_solution = backward_solve(mid_inverse, mid_back_in, 2)
    mid_local = row_tiles(mid_solution.astype(jnp.bfloat16))
    ancestors = jnp.concatenate([mid_local, top_local], axis=0)
    leaf_return = couple_backward(leaf_slab, leaf_targets[0, 0], leaf_counts[0, 0], ancestors)
    leaf_back = (leaf_forward - leaf_return).astype(jnp.bfloat16)
    leaf_solution = backward_solve(leaf_inverse, leaf_back, 1)
    return (
        leaf_solution.reshape(leaf_rhs.shape),
        mid_solution.reshape(leaf_rhs.shape),
        top_solution.reshape(leaf_rhs.shape),
    )


def solution(mesh):
    placed = (
        P("leaf", "row", "col", None, None, None),
        P("leaf", "row", "col", None, None, None),
        P("leaf", "row", "col", None, None, None),
        P("leaf", "row", None, None, "col", None, None),
        P("leaf", "row", None, None, "col", None, None),
        P("leaf", "row", None, None, "col", None, None),
        P("leaf", "row", None, None, None, "col", None, None),
        P("leaf", "row", None, None, None, "col", None, None),
        P("leaf", "row", None, None),
        P("leaf", "row", None),
        P("leaf", "row", None, None),
        P("leaf", "row", None),
    )
    return jax.shard_map(
        shards,
        mesh=mesh,
        in_specs=placed,
        out_specs=(
            P("leaf", "row", "col", None, None, None),
            P("leaf", "row", "col", None, None, None),
            P("leaf", "row", "col", None, None, None),
        ),
        check_vma=False,
    )
```

profile of v0, /device:TPU:1, one launch (start us, length us, event | category | flops | bytes accessed | tf_op | source)
XLA Modules:
  0.0 879.0 jit_solution(12042325339444213601)
XLA Ops:
  7.2 1.5 convert_element_type.202
  8.8 49.7 %all-gather.14.cloned.1.call-done = bf16[32,1,1,1,128,256]{5,4,3,2,1,0:T(8,128)(2,1)} async-done(((bf16[1,1,1,1,128,256]{5,4,3,2,1,0:T(8,128)(2,1)}), bf16[32,1,1,1,128,256]{5,4,3,2,1,0:T(8,128)(2,1)}) %all-gather.14.cloned.1.call-update) | async-done | bytes 2097168 | tf_op jit(solution)/shard_map/all_gather | solution.py:32
  58.5 1.1 constant_dynamic-slice_fusion.1
  59.6 1.7 fusion.38
  62.2 17.2 %reduce-scatter.11.cloned.1.call-done = bf16[1,1,1,128,256]{4,3,2,1,0:T(8,128)(2,1)} async-done(((bf16[1,4,1,128,256]{4,3,2,1,0:T(8,128)(2,1)}), bf16[1,1,1,128,256]{4,3,2,1,0:T(8,128)(2,1)}) %reduce-scatter.11.cloned.1.call-update) | async-done | bytes 65552 | tf_op jit(solution)/shard_map/reduce_scatter | solution.py:39
  79.5 10.3 %reshape_squeeze.8 = bf16[4,768,1024]{2,1,0:T(8,128)(2,1)} reshape(bf16[1,1,4,6,128,1,8,128]{7,6,5,4,3,2,1,0:T(8,128)(2,1)} %param.18) | data formatting | bytes 12582912 | tf_op jit(solution)/shard_map/reshape;squeeze | solution.py:86
  89.9 38.5 %all-gather.16.cloned.1.call-done = bf16[32,1,1,128,256]{4,3,2,1,0:T(8,128)(2,1)} async-done(((bf16[1,1,1,128,256]{4,3,2,1,0:T(8,128)(2,1)}), bf16[32,1,1,128,256]{4,3,2,1,0:T(8,128)(2,1)}) %all-gather.16.cloned.1.call-update) | async-done | bytes 2097168 | tf_op jit(solution)/shard_map/all_gather | solution.py:32
  128.4 7.1 convolution_bitcast_fusion.1
  135.5 2.4 copy.44
  137.9 2.6 reshape.414
  140.5 3.3 reshape.475
  143.7 4.9 fusion.24
  149.6 18.6 %reduce-scatter.13.cloned.1.call-done = bf16[2,1,1,128,256]{4,3,2,0,1:T(8,128)(2,1)} async-done(((bf16[2,4,1,128,256]{4,3,2,0,1:T(8,128)(2,1)}), bf16[2,1,1,128,256]{4,3,2,0,1:T(8,128)(2,1)}) %reduce-scatter.13.cloned.1.call-update) | async-done | bytes 131088 | tf_op jit(solution)/shard_map/reduce_scatter | solution.py:39
  168.2 0.9 convert_element_type.209
  169.9 47.1 %all-gather.10.cloned.1.call-done = bf16[32,128,256]{2,1,0:T(8,128)(2,1)} async-done(((bf16[1,128,256]{2,1,0:T(8,128)(2,1)}), bf16[32,128,256]{2,1,0:T(8,128)(2,1)}) %all-gather.10.cloned.1.call-update) | async-done | bytes 2097168 | tf_op jit(solution)/shard_map/all_gather | solution.py:32
  217.0 1.3 constant_dynamic-slice_fusion
  218.3 2.4 fusion.35
  221.6 17.2 %reduce-scatter.15.cloned.1.call-done = bf16[1,1,1,128,256]{4,3,2,1,0:T(8,128)(2,1)} async-done(((bf16[1,4,1,128,256]{4,3,2,1,0:T(8,128)(2,1)}), bf16[1,1,1,128,256]{4,3,2,1,0:T(8,128)(2,1)}) %reduce-scatter.15.cloned.1.call-update) | async-done | bytes 65552 | tf_op jit(solution)/shard_map/reduce_scatter | solution.py:39
  239.1 7.4 reshape_squeeze.9
  246.5 41.0 %all-gather.18.cloned.1.call-done = bf16[32,1,1,128,256]{4,3,2,1,0:T(8,128)(2,1)} async-done(((bf16[1,1,1,128,256]{4,3,2,1,0:T(8,128)(2,1)}), bf16[32,1,1,128,256]{4,3,2,1,0:T(8,128)(2,1)}) %all-gather.18.cloned.1.call-update) | async-done | bytes 2097168 | tf_op jit(solution)/shard_map/all_gather | solution.py:32
  287.5 4.4 convolution_bitcast_fusion.3
  292.8 0.9 fusion.34
  294.5 17.2 %reduce-scatter.17.cloned.1.call-done = bf16[1,1,1,128,256]{4,3,2,0,1:T(8,128)(2,1)} async-done(((bf16[1,4,1,128,256]{4,3,2,0,1:T(8,128)(2,1)}), bf16[1,1,1,128,256]{4,3,2,0,1:T(8,128)(2,1)}) %reduce-scatter.17.cloned.1.call-update) | async-done | bytes 65552 | tf_op jit(solution)/shard_map/reduce_scatter | solution.py:39
  311.7 1.5 fusion.57
  313.3 48.0 %all-gather.12.cloned.1.call-done = bf16[32,128,256]{2,1,0:T(8,128)(2,1)} async-done(((bf16[1,128,256]{2,1,0:T(8,128)(2,1)}), bf16[32,128,256]{2,1,0:T(8,128)(2,1)}) %all-gather.12.cloned.1.call-update) | async-done | bytes 2097168 | tf_op jit(solution)/shard_map/all_gather | solution.py:32
  361.3 5.6 fusion.39
  367.7 17.2 %reduce-scatter.19.cloned.1.call-done = bf16[1,1,1,128,256]{4,3,2,1,0:T(8,128)(2,1)} async-done(((bf16[1,4,1,128,256]{4,3,2,1,0:T(8,128)(2,1)}), bf16[1,1,1,128,256]{4,3,2,1,0:T(8,128)(2,1)}) %reduce-scatter.19.cloned.1.call-update) | async-done | bytes 65552 | tf_op jit(solution)/shard_map/reduce_scatter | solution.py:39
  385.0 10.0 %all-gather.3 = bf16[4,1,1,128,256]{4,3,2,1,0:T(8,128)(2,1)S(1)} all-gather(bf16[1,1,1,128,256]{4,3,2,1,0:T(8,128)(2,1)} %reduce-scatter.19.cloned.1.call-done), channel_id=5, replica_groups=mesh['leaf'=4,'row'=8,'col'=4] {'col'}, dimensions={0}, use_global_device_ids=true | all-gather | bytes 327680 | tf_op jit(solution)/shard_map/all_gather | solution.py:44
  395.0 3.9 fusion
  398.9 2.5 copy.75
  401.7 81.7 %reduce-scatter.21.cloned.1.call-done = bf16[1,128,256]{2,1,0:T(8,128)(2,1)} async-done(((bf16[32,128,256]{2,1,0:T(8,128)(2,1)}), bf16[1,128,256]{2,1,0:T(8,128)(2,1)}) %reduce-scatter.21.cloned.1.call-update) | async-done | bytes 65552 | tf_op jit(solution)/shard_map/reduce_scatter | solution.py:47
  483.5 9.9 %all_gather.36 = bf16[4,128,256]{2,1,0:T(8,128)(2,1)S(1)} all-gather(bf16[1,128,256]{2,1,0:T(8,128)(2,1)} %reduce-scatter.21.cloned.1.call-done), channel_id=1, replica_groups=mesh['leaf'=4,'row'=8,'col'=4] {'col'}, dimensions={0}, use_global_device_ids=true | all-gather | bytes 327680 | tf_op jit(solution)/shard_map/all_gather | solution.py:44
  494.1 3.4 fusion.9
  497.6 2.5 copy.58
  500.2 80.7 %reduce-scatter.23.cloned.1.call-done = bf16[1,128,256]{2,1,0:T(8,128)(2,1)} async-done(((bf16[32,128,256]{2,1,0:T(8,128)(2,1)}), bf16[1,128,256]{2,1,0:T(8,128)(2,1)}) %reduce-scatter.23.cloned.1.call-update) | async-done | bytes 65552 | tf_op jit(solution)/shard_map/reduce_scatter | solution.py:47
  581.7 9.7 %all_gather.37 = bf16[4,128,256]{2,1,0:T(8,128)(2,1)S(1)} all-gather(bf16[1,128,256]{2,1,0:T(8,128)(2,1)S(1)} %fusion.60), channel_id=1, replica_groups=mesh['leaf'=4,'row'=8,'col'=4] {'col'}, dimensions={0}, use_global_device_ids=true | all-gather | bytes 327680 | tf_op jit(solution)/shard_map/all_gather | solution.py:44
  591.4 2.3 convolution_bitcast_fusion
  594.6 1.4 copy-done.1
  596.4 80.2 %reduce-scatter.25.cloned.1.call-done = bf16[1,128,256]{2,1,0:T(8,128)(2,1)} async-done(((bf16[32,128,256]{2,1,0:T(8,128)(2,1)}), bf16[1,128,256]{2,1,0:T(8,128)(2,1)}) %reduce-scatter.25.cloned.1.call-update) | async-done | bytes 65552 | tf_op jit(solution)/shard_map/reduce_scatter | solution.py:47
  676.7 10.1 %all_gather.38 = bf16[4,128,256]{2,1,0:T(8,128)(2,1)S(1)} all-gather(bf16[1,128,256]{2,1,0:T(8,128)(2,1)} %reduce-scatter.25.cloned.1.call-done), channel_id=1, replica_groups=mesh['leaf'=4,'row'=8,'col'=4] {'col'}, dimensions={0}, use_global_device_ids=true | all-gather | bytes 327680 | tf_op jit(solution)/shard_map/all_gather | solution.py:44
  687.5 1.6 copy.60
  689.0 5.1 convert_bitcast_fusion
  694.1 2.6 copy.61
  696.8 80.6 %reduce-scatter.27.cloned.1.call-done = bf16[1,128,256]{2,1,0:T(8,128)(2,1)} async-done(((bf16[32,128,256]{2,1,0:T(8,128)(2,1)}), bf16[1,128,256]{2,1,0:T(8,128)(2,1)}) %reduce-scatter.27.cloned.1.call-update) | async-done | bytes 65552 | tf_op jit(solution)/shard_map/reduce_scatter | solution.py:47
  778.3 9.7 %all_gather.39 = bf16[4,128,256]{2,1,0:T(8,128)(2,1)S(1)} all-gather(bf16[1,128,256]{2,1,0:T(8,128)(2,1)S(1)} %fusion.61), channel_id=1, replica_groups=mesh['leaf'=4,'row'=8,'col'=4] {'col'}, dimensions={0}, use_global_device_ids=true | all-gather | bytes 327680 | tf_op jit(solution)/shard_map/all_gather | solution.py:44
  789.0 1.3 copy-done
  791.7 79.3 %reduce-scatter.29.cloned.1.call-done = bf16[1,128,256]{2,1,0:T(8,128)(2,1)} async-done(((bf16[32,128,256]{2,1,0:T(8,128)(2,1)}), bf16[1,128,256]{2,1,0:T(8,128)(2,1)}) %reduce-scatter.29.cloned.1.call-update) | async-done | bytes 65552 | tf_op jit(solution)/shard_map/reduce_scatter | solution.py:47
  871.0 1.5 bitcast_convert_fusion.2
  (97 shorter events, 13.8 us)
Async XLA Ops:
  7.2 51.3 %all-gather.14.cloned.1.call-start = ((), (), s32[]{:S(2)}) async-start(), calls=%async_computation.22 | async-start | bytes 2162688 | tf_op jit(solution)/shard_map/all_gather | solution.py:32
  8.8 70.7 %reduce-scatter.11.cloned.1.call-start = ((), (), s32[]{:S(2)}) async-start(), calls=%async_computation.10 | async-start | bytes 327680 | tf_op jit(solution)/shard_map/reduce_scatter | solution.py:39
  62.2 66.2 %all-gather.16.cloned.1.call-start = ((), (), s32[]{:S(2)}) async-start(), calls=%async_computation.23 | async-start | bytes 2162688 | tf_op jit(solution)/shard_map/all_gather | solution.py:32
  79.5 10.4 %copy-start.12 = (s32[1,1,4]{2,1,0:T(1,128)S(1)}, s32[1,1,4]{2,1,0:T(1,128)}, u32[]{:S(2)}) copy-start(s32[1,1,4]{2,1,0:T(1,128)} %param.21) | copy-start | bytes 52
  79.5 88.7 %reduce-scatter.13.cloned.1.call-start = ((), (), s32[]{:S(2)}) async-start(), calls=%async_computation.11 | async-start | bytes 655360 | tf_op jit(solution)/shard_map/reduce_scatter | solution.py:39
  140.5 3.3 copy-start.8
  143.7 25.4 %copy-start.7 = (f32[1,1,1,1,128,256]{5,4,3,2,1,0:T(8,128)S(1)}, f32[1,1,1,1,128,256]{5,4,3,2,1,0:T(8,128)}, u32[]{:S(2)}) copy-start(f32[1,1,1,1,128,256]{5,4,3,2,1,0:T(8,128)} %param.13) | copy-start | bytes 393220
  149.5 67.5 %all-gather.10.cloned.1.call-start = ((), (), s32[]{:S(2)}) async-start(), calls=%async_computation.12 | async-start | bytes 2162688 | tf_op jit(solution)/shard_map/all_gather | solution.py:32
  169.8 69.0 %reduce-scatter.15.cloned.1.call-start = ((), (), s32[]{:S(2)}) async-start(), calls=%async_computation.13 | async-start | bytes 327680 | tf_op jit(solution)/shard_map/reduce_scatter | solution.py:39
  221.5 66.0 %all-gather.18.cloned.1.call-start = ((), (), s32[]{:S(2)}) async-start(), calls=%async_computation.24 | async-start | bytes 2162688 | tf_op jit(solution)/shard_map/all_gather | solution.py:32
  238.8 7.6 copy-start.11
  238.9 72.9 %reduce-scatter.17.cloned.1.call-start = ((), (), s32[]{:S(2)}) async-start(), calls=%async_computation.14 | async-start | bytes 327680 | tf_op jit(solution)/shard_map/reduce_scatter | solution.py:39
  291.9 0.9 copy-start.9
  292.2 19.5 %copy-start.6 = (f32[1,1,1,1,128,256]{5,4,3,2,1,0:T(8,128)S(1)}, f32[1,1,1,1,128,256]{5,4,3,2,1,0:T(8,128)}, u32[]{:S(2)}) copy-start(f32[1,1,1,1,128,256]{5,4,3,2,1,0:T(8,128)} %param.14) | copy-start | bytes 393220
  294.5 66.8 %all-gather.12.cloned.1.call-start = ((), (), s32[]{:S(2)}) async-start(), calls=%async_computation.15 | async-start | bytes 2162688 | tf_op jit(solution)/shard_map/all_gather | solution.py:32
  313.3 71.7 %reduce-scatter.19.cloned.1.call-start = ((), (), s32[]{:S(2)}) async-start(), calls=%async_computation.16 | async-start | bytes 327680 | tf_op jit(solution)/shard_map/reduce_scatter | solution.py:39
  367.7 115.8 %reduce-scatter.21.cloned.1.call-start = ((), (), s32[]{:S(2)}) async-start(), calls=%async_computation.17 | async-start | bytes 2162688 | tf_op jit(solution)/shard_map/reduce_scatter | solution.py:47
  401.4 179.4 %reduce-scatter.23.cloned.1.call-start = ((), (), s32[]{:S(2)}) async-start(), calls=%async_computation.18 | async-start | bytes 2162688 | tf_op jit(solution)/shard_map/reduce_scatter | solution.py:47
  500.1 80.7 %copy-start.5 = (bf16[1,1,1,128,256]{4,3,2,1,0:T(8,128)(2,1)S(1)}, bf16[1,1,1,128,256]{4,3,2,1,0:T(8,128)(2,1)}, u32[]{:S(2)}) copy-start(bf16[1,1,1,128,256]{4,3,2,1,0:T(8,128)(2,1)} %reduce-scatter.15.cloned.1.call-done) | copy-start | bytes 196612
  500.1 176.5 %reduce-scatter.25.cloned.1.call-start = ((), (), s32[]{:S(2)}) async-start(), calls=%async_computation.19 | async-start | bytes 2162688 | tf_op jit(solution)/shard_map/reduce_scatter | solution.py:47
  594.6 1.4 copy-start.1
  596.0 181.4 %reduce-scatter.27.cloned.1.call-start = ((), (), s32[]{:S(2)}) async-start(), calls=%async_computation.20 | async-start | bytes 2162688 | tf_op jit(solution)/shard_map/reduce_scatter | solution.py:47
  696.7 80.7 %copy-start.4 = (bf16[1,1,1,128,256]{4,3,2,1,0:T(8,128)(2,1)S(1)}, bf16[1,1,1,128,256]{4,3,2,1,0:T(8,128)(2,1)}, u32[]{:S(2)}) copy-start(bf16[1,1,1,128,256]{4,3,2,1,0:T(8,128)(2,1)} %reduce-scatter.11.cloned.1.call-done) | copy-start | bytes 196612
  696.7 91.3 %copy-start.10 = (bf16[1,1,4,128,1,8,128]{6,5,4,3,2,1,0:T(8,128)(2,1)S(1)}, bf16[1,1,4,128,1,8,128]{6,5,4,3,2,1,0:T(8,128)(2,1)}, u32[]{:S(2)}) copy-start(bf16[1,1,4,128,1,8,128]{6,5,4,3,2,1,0:T(8,128)(2,1)} %param.15) | copy-start | bytes 3145732
  696.7 174.3 %reduce-scatter.29.cloned.1.call-start = ((), (), s32[]{:S(2)}) async-start(), calls=%async_computation.21 | async-start | bytes 2162688 | tf_op jit(solution)/shard_map/reduce_scatter | solution.py:47
  788.9 1.4 copy-start.2
  788.9 2.1 copy-start.3
  789.0 1.3 copy-start
Sparse Core Ops, SparseCore 0:
  10.8 47.6 all-gather.13
  62.3 17.1 reduce-scatter.10
  82.0 46.3 all-gather.15
  149.7 18.4 reduce-scatter.12
  171.1 45.8 all-gather.9
  221.6 17.1 reduce-scatter.14
  241.1 46.3 all-gather.17
  294.6 17.1 reduce-scatter.16
  314.8 46.3 all-gather.11
  367.8 17.1 reduce-scatter.18
  401.5 81.8 reduce-scatter.20
  500.3 80.5 reduce-scatter.22
  596.1 80.4 reduce-scatter.24
  696.9 80.5 reduce-scatter.26
  790.4 80.5 reduce-scatter.28
where the time goes:
time: 881 us; the launch traced here: 879 us
  waiting for transfers between devices  715 us (81%)
  blocking collectives  49.3 us (6%)
  local copies, waits for them, and re-layouts  48.5 us (6%)
  matrix products  42.1 us (5%)
  between operations  14.3 us (2%)
  other arithmetic  9.45 us (1%)
    reduce_scatter x5, waiting for transfers between devices, group_sum(): lax.psum_scatter(partial_value.astype(jnp.bfloat16), ('leaf', 'row'), sca...  403 us
    all_gather x5, waiting for transfers between devices, gather_all(): return lax.all_gather(vector, ('leaf', 'row'), axis=0, tiled=True)  224 us
    reduce_scatter x5, waiting for transfers between devices, column_sum(): lax.psum_scatter(stacked.astype(jnp.bfloat16), 'col', scatter_dimension=1...  87.6 us
    all_gather x5, blocking collectives, row_tiles(): return lax.all_gather(vector, 'col', axis=0, tiled=True)  49.3 us
    another operation x2, local copies, waits for them, and re-layouts, couple_backward(): matrix = coupling.reshape(sources, slot_count * tile_rows, -1)  17.7 us
  transfers between devices with their start and end apart: 15, of which 15 were waited for; matrix products, arithmetic and copies ran while one was open for 2% of the time, Pallas kernels for 0%

commit v1 on v0

v1 whole, which is shorter than its diff:
```python
import functools

import jax
import jax.numpy as jnp
from jax import lax
from jax.experimental import pallas as pl
from jax.experimental.pallas import tpu as pltpu
from jax.sharding import PartitionSpec as P

MESH = pl.DeviceIdType.MESH
TILE = 128
GROUP = 4 * TILE
CHAINS = 2
BF = jnp.bfloat16
F32 = jnp.float32


def kernel(
    width,
    leaf_rhs,
    mid_rhs,
    top_rhs,
    leaf_inv,
    mid_inv,
    top_inv,
    leaf_cpl,
    mid_cpl,
    leaf_tgt,
    leaf_cnt,
    mid_tgt,
    mid_cnt,
    leaf_out,
    mid_out,
    top_out,
    st_li,
    st_lc0,
    st_lc1,
    st_16a,
    st_16b,
    st_ti,
    wl,
    wm,
    wt,
    gm,
    gt,
    hm,
    x1,
    x2,
    x3,
    x4,
    x5,
    pf,
    xs,
    xr,
    top_part,
    yt,
    sib_s,
    pl_s,
    sib_r0,
    sib_r1,
    sib_r2,
    pl_r0,
    pl_r1,
    pl_r3,
    pl_r4,
    pl_r5,
    own,
    top_acc,
    lf,
    mf,
    w_sem,
    ag_rx,
    ag_rxs,
    ag_tx,
    ag_txs,
    x_rx,
    x_tx,
    rs_rx,
    rs_rxs,
    rs_tx,
    rs_txs,
):
    y = lax.axis_index("leaf")
    row = lax.axis_index("row")
    c = lax.axis_index("col")
    z, e = lax.div(row, 2), lax.rem(row, 2)
    eo = 1 - e
    half = lax.div(y, 2)
    par = lax.rem(y, 2)

    def partners(a):
        near = a + 1 - 2 * lax.rem(a, 2)
        return [a, near, lax.rem(a + 2, 4), lax.rem(near + 2, 4)]

    ys, zs, cs = partners(y), partners(z), partners(c)
    pars = [par, 1 - par]
    sibling = (y, z * 2 + eo, c)

    def plane(dy, dz):
        return (ys[dy], zs[dz] * 2 + e, c)

    srcs = [2 * half, 2 * half + 1, 2 * (1 - half), 2 * (1 - half) + 1]
    fetch = {
        "li": pltpu.make_async_copy(leaf_inv, st_li, w_sem.at[0]),
        "lc0": pltpu.make_async_copy(leaf_cpl.at[srcs[0]], st_lc0, w_sem.at[1]),
        "lc1": pltpu.make_async_copy(leaf_cpl.at[srcs[1]], st_lc1, w_sem.at[2]),
        "mi": pltpu.make_async_copy(mid_inv, st_16a, w_sem.at[3]),
        "lc2": pltpu.make_async_copy(leaf_cpl.at[srcs[2]], st_lc0, w_sem.at[4]),
        "lc3": pltpu.make_async_copy(leaf_cpl.at[srcs[3]], st_lc1, w_sem.at[5]),
        "hm0": pltpu.make_async_copy(mid_cpl.at[0], st_16b, w_sem.at[6]),
        "hm1": pltpu.make_async_copy(mid_cpl.at[1], st_16a, w_sem.at[7]),
        "ti": pltpu.make_async_copy(top_inv, st_ti, w_sem.at[8]),
    }
    for name in ("li", "lc0", "lc1", "mi", "hm0", "ti"):
        fetch[name].start()

    def by_core(x, first, core):
        at = [(first + 2 * k + core) * TILE for k in range(4)]
        return jnp.concatenate([x[:, a : a + TILE] for a in at], axis=1)

    def lay_inverse(name, stage, dst, groups):
        fetch[name].wait()
        for q in range(4):
            rows = slice(q * TILE, (q + 1) * TILE)
            x = stage[rows].reshape(TILE, groups * 8 * TILE)
            for g in range(groups):
                for core in range(2):
                    dst[core, g, rows, :] = by_core(x, g * 8, core)

    def find_slot(targets, counts, k, v, slots):
        at, live = jnp.int32(0), jnp.int32(0)
        for m in range(slots):
            hit = jnp.logical_and(targets[k, m] == v, m < counts[k])
            at = jnp.where(hit, m, at)
            live = jnp.where(hit, 1, live)
        return at, live

    def lay_slot(x, live, width_tiles):
        x = x.reshape(TILE, width_tiles * TILE)
        return x * jnp.full(x.shape, live.astype(F32), F32).astype(BF)

    def lay_leaf_coupling(j):
        k = srcs[j]
        fetch[f"lc{j}"].wait()
        for v in range(0 if j < 2 else 4, 8):
            at, live = find_slot(leaf_tgt, leaf_cnt, k, v, 6)
            x = lay_slot((st_lc0, st_lc1)[j % 2][at], live, 8)
            rows = slice(v % 4 * TILE, (v % 4 + 1) * TILE)
            for core in range(2):
                if v < 4:
                    gm[core, j, rows, :] = by_core(x, 0, core)
                else:
                    gt[core, k, rows, :] = by_core(x, 0, core)
        if j < 2:
            fetch[f"lc{j + 2}"].start()

    def lay_mid_inverse():
        fetch["mi"].wait()
        for q in range(4):
            rows = slice(q * TILE, (q + 1) * TILE)
            x = st_16a[q].reshape(TILE, 16 * TILE)
            for g in range(2):
                for core in range(2):
                    wm[core, g, rows, :] = by_core(x, g * 8, core)
        fetch["hm1"].start()

    def lay_mid_coupling(k):
        fetch[f"hm{k}"].wait()
        for v in range(4):
            at, live = find_slot(mid_tgt, mid_cnt, k, v, 4)
            x = lay_slot((st_16b, st_16a)[k][at], live, 16)
            rows = slice(v * TILE, (v + 1) * TILE)
            for g in range(2):
                for core in range(2):
                    hm[core, 2 * k + g, rows, :] = by_core(x, g * 8, core)

    tasks = {
        0: [lambda: lay_inverse("li", st_li, wl, 1)],
        1: [lambda: lay_leaf_coupling(0), lambda: lay_leaf_coupling(1)],
        2: [lay_mid_inverse, lambda: lay_leaf_coupling(2)],
        3: [lambda: lay_leaf_coupling(3), lambda: lay_mid_coupling(0)],
        4: [lambda: lay_mid_coupling(1)],
        5: [lambda: lay_inverse("ti", st_ti, wt, 4)],
    }

    barrier = pltpu.get_barrier_semaphore()
    reached = [sibling] + [plane(a, b) for a in range(4) for b in range(4) if a or b]
    reached += [(y, row, cs[k]) for k in range(1, 4)]
    for device in reached:
        pl.semaphore_signal(barrier, inc=1, device_id=device, device_id_type=MESH)
    pl.semaphore_wait(barrier, len(reached))

    def remote(src, dst, tx, rx, device):
        return pltpu.make_async_remote_copy(
            src_ref=src, dst_ref=dst, send_sem=tx, recv_sem=rx, device_id=device, device_id_type=MESH
        )

    def chain(h):
        sent = []
        cols = slice(h * width, (h + 1) * width)

        def drain():
            for ref, sem in sent:
                remote(ref, ref, sem, sem, sibling).wait_send()
            sent.clear()

        def arrived(ref, sem):
            remote(ref, ref, sem, sem, sibling).wait_recv()

        def gather_send(ph, x, at, value, dys):
            mine = x.at[h, e, at[0], pl.ds(z * TILE, TILE)]
            x[h, e, at[0], pl.ds(z * TILE, TILE), :] = value
            for dy in dys:
                for dz in (2, 1, 3, 0):
                    if dy or dz:
                        remote(mine, mine, ag_tx.at[ph, h, dy], ag_rx.at[ph, h, dy], plane(dy, dz)).start()
                tiles = 4 if dy else 3
                sent.append((x.at[h, 0, 0, pl.ds(0, tiles * TILE)], ag_tx.at[ph, h, dy]))

        def gather_forward(ph, x, at, dy):
            tiles = 4 if dy else 3
            arrived(x.at[h, e, at[dy], pl.ds(0, tiles * TILE)], ag_rx.at[ph, h, dy])
            block = x.at[h, e, at[dy]]
            remote(block, block, ag_txs.at[ph, h, dy], ag_rxs.at[ph, h, dy], sibling).start()
            sent.append((block, ag_txs.at[ph, h, dy]))

        def gather_done(ph, x, at, dy):
            arrived(x.at[h, eo, at[dy]], ag_rxs.at[ph, h, dy])

        def products(w, wat, x, at, core, dys):
            total = None
            for dy in dys:
                part = jnp.dot(w[core, wat[dy]], x[h, core, at[dy]], preferred_element_type=F32)
                total = part if total is None else total + part
            return total

        def gathered_product(ph, w, wat, x, at, dys):
            for dy in dys:
                gather_forward(ph, x, at, dy)
            total = products(w, wat, x, at, e, dys)
            for dy in dys:
                gather_done(ph, x, at, dy)
            return total + products(w, wat, x, at, eo, dys)

        def column_send(ph, total):
            for q in range(4):
                tile = total[q * TILE : (q + 1) * TILE]
                pf[h, q] = tile
                xs[ph, h, q] = tile.astype(BF)
            for dc in (2, 1, 3):
                remote(
                    xs.at[ph, h, cs[dc]], xr.at[ph, h, dc - 1], x_tx.at[ph, h], x_rx.at[ph, h], (y, row, cs[dc])
                ).start()
            sent.append((xs.at[ph, h, pl.ds(0, 3)], x_tx.at[ph, h]))

        def column_sum(ph):
            arrived(xr.at[ph, h], x_rx.at[ph, h])
            total = pf[h, c]
            for k in range(3):
                total = total + xr[ph, h, k].astype(F32)
            return total

        def row_send(ph, value):
            mine = yt.at[ph, h, c]
            yt[ph, h, c] = value
            for dc in (2, 1, 3):
                remote(mine, mine, x_tx.at[5 + ph, h], x_rx.at[5 + ph, h], (y, row, cs[dc])).start()
            sent.append((yt.at[ph, h, pl.ds(0, 3)], x_tx.at[5 + ph, h]))

        def row_tiles(ph):
            arrived(yt.at[ph, h, pl.ds(0, 3)], x_rx.at[5 + ph, h])
            return jnp.concatenate([yt[ph, h, q] for q in range(4)], axis=1)

        def group_send(ph, piece, s_at, sib_r, r_at, pl_r, dys):
            for k, dy in enumerate(dys):
                sib_s[s_at, h, dy] = piece(0, dy).astype(BF)
                remote(
                    sib_s.at[s_at, h, dy], sib_r.at[r_at, h, dy], rs_txs.at[ph, h, dy], rs_rxs.at[ph, h, dy], sibling
                ).start()
                sent.append((sib_s.at[s_at, h, dy], rs_txs.at[ph, h, dy]))
            for dy in dys:
                total = piece(1, dy)
                arrived(sib_r.at[r_at, h, dy], rs_rxs.at[ph, h, dy])
                total = total + sib_r[r_at, h, dy].astype(F32)
                for k in range(4):
                    tile = total[:, k * TILE : (k + 1) * TILE]
                    pl_s[s_at, h, dy * 4 + k] = tile.astype(BF)
                    if dy == 0:
                        own[h, k] = tile
                for dz in (2, 1, 3, 0):
                    if dy or dz:
                        remote(
                            pl_s.at[s_at, h, dy * 4 + zs[dz]],
                            pl_r.at[h, dy * 4 + dz],
                            rs_tx.at[ph, h, dy],
                            rs_rx.at[ph, h],
                            plane(dy, dz),
                        ).start()
                tiles = 4 if dy else 3
                sent.append((pl_s.at[s_at, h, pl.ds(0, tiles)], rs_tx.at[ph, h, dy]))

        def group_sum(ph, pl_r, tiles):
            arrived(pl_r.at[h, pl.ds(1, tiles)], rs_rx.at[ph, h])
            total = own[h, z]
            for k in range(1, tiles + 1):
                total = total + pl_r[h, k].astype(F32)
            return total

        zero = [0]
        far = (2, 1, 3, 0)

        gather_send(0, x1, zero, leaf_rhs[:, cols].astype(BF), (0,))
        yield
        column_send(0, gathered_product(0, wl, zero, x1, zero, (0,)))
        yield
        drain()
        forward = column_sum(0)
        gather_send(1, x2, ys, forward.astype(BF), (1, 0, 2, 3))
        lf[h] = forward.T
        yield
        column_send(1, gathered_product(1, gm, pars, x2, ys, (0, 1)))
        yield
        drain()
        gather_send(2, x3, pars, (mid_rhs[:, cols] - column_sum(1)).astype(BF), (1, 0))
        for dy in (3, 2):
            gather_forward(1, x2, ys, dy)
        yield
        column_send(2, gathered_product(2, wm, pars, x3, pars, (0, 1)))
        for dy in (3, 2):
            gather_done(1, x2, ys, dy)
        top_part[h] = products(gt, ys, x2, ys, e, far) + products(gt, ys, x2, ys, eo, far)
        yield
        drain()
        forward = column_sum(2)
        gather_send(3, x4, ys, forward.astype(BF), far)
        mf[h] = forward.T
        yield
        column_send(3, gathered_product(3, hm, ys, x4, ys, (0, 1, 3, 2)) + top_part[h])
        yield
        drain()
        gather_send(4, x5, ys, (top_rhs[:, cols] - column_sum(3)).astype(BF), far)
        yield
        column_send(4, gathered_product(4, wt, ys, x5, ys, (0, 1, 3, 2)))
        yield
        drain()
        row_send(0, column_sum(4).T.astype(BF))
        yield

        def both(w, wat, values):
            def piece(mine, dy):
                return jnp.dot(values, w[e if mine else eo, wat[dy]], preferred_element_type=F32)

            return piece

        values = row_tiles(0)
        group_send(0, both(wt, ys, values), 0, sib_r0, 0, pl_r0, far)
        yield
        drain()
        solution_t = group_sum(0, pl_r0, 15)
        row_send(1, solution_t.astype(BF))
        top_out[:, cols] = solution_t.T
        yield
        values = row_tiles(1)
        group_send(1, both(hm, ys, values), 1, sib_r0, 1, pl_r1, far)
        part = both(gt, ys, values)
        for mine in range(2):
            for dy in range(2):
                top_acc[h, mine, dy] = part(mine, dy)
        yield
        drain()
        row_send(2, (mf[h] - group_sum(1, pl_r1, 15)).astype(BF))
        group_send(2, part, 0, sib_r0, 2, pl_r4, (2, 3))
        yield
        values = row_tiles(2)
        group_send(3, both(wm, pars, values), 1, sib_r1, 0, pl_r3, (1, 0))
        yield
        drain()
        solution_t = group_sum(3, pl_r3, 7)
        row_send(3, solution_t.astype(BF))
        mid_out[:, cols] = solution_t.T
        arrived(pl_r4.at[h, pl.ds(8, 8)], rs_rx.at[2, h])
        late = lf[h]
        for k in range(8, 16):
            late = late - pl_r4[h, k].astype(F32)
        lf[h] = late
        yield
        values = row_tiles(3)
        mid_piece = both(gm, pars, values)
        group_send(
            4, lambda mine, dy: mid_piece(mine, dy) + top_acc[h, mine, dy], 0, sib_r1, 1, pl_r4, (1, 0)
        )
        yield
        drain()
        row_send(4, (lf[h] - group_sum(4, pl_r4, 7)).astype(BF))
        yield
        values = row_tiles(4)
        group_send(5, both(wl, zero, values), 1, sib_r2, 0, pl_r5, (0,))
        yield
        drain()
        leaf_out[:, cols] = group_sum(5, pl_r5, 3).T
        drain()

    running = [chain(h) for h in range(CHAINS)]
    step = 0
    while running:
        alive = []
        for g in running:
            if next(g, "end") != "end":
                alive.append(g)
        running = alive
        for task in tasks.get(step, ()):
            task()
        step += 1


def shards(
    leaf_rhs,
    mid_rhs,
    top_rhs,
    leaf_inverse,
    mid_inverse,
    top_inverse,
    leaf_coupling,
    mid_coupling,
    leaf_targets,
    leaf_counts,
    mid_targets,
    mid_counts,
):
    shape = leaf_rhs.shape
    rhs = shape[-1]
    n = rhs // CHAINS
    h = CHAINS
    vmem = pl.BlockSpec(memory_space=pltpu.VMEM)
    smem = pl.BlockSpec(memory_space=pltpu.SMEM)
    hbm = pl.BlockSpec(memory_space=pl.ANY)
    out = jax.ShapeDtypeStruct((TILE, rhs), F32)
    dma = pltpu.SemaphoreType.DMA
    weights = [pltpu.VMEM((2, k, GROUP, GROUP), BF) for k in (1, 2, 4, 2, 4, 4)]
    vectors = [pltpu.VMEM((h, 2, k, GROUP, n), BF) for k in (1, 4, 2, 4, 4)]
    outs = pl.pallas_call(
        functools.partial(kernel, n),
        out_shape=(out, out, out),
        in_specs=[vmem] * 3 + [hbm] * 5 + [smem] * 4,
        out_specs=(vmem, vmem, vmem),
        scratch_shapes=[
            pltpu.VMEM((GROUP, 8, TILE), BF),
            pltpu.VMEM((6, TILE, 8, TILE), BF),
            pltpu.VMEM((6, TILE, 8, TILE), BF),
            pltpu.VMEM((4, TILE, 16, TILE), BF),
            pltpu.VMEM((4, TILE, 16, TILE), BF),
            pltpu.VMEM((GROUP, 32, TILE), BF),
            *weights,
            *vectors,
            pltpu.VMEM((h, 4, TILE, n), F32),
            pltpu.VMEM((5, h, 4, TILE, n), BF),
            pltpu.VMEM((5, h, 3, TILE, n), BF),
            pltpu.VMEM((h, GROUP, n), F32),
            pltpu.VMEM((5, h, 4, n, TILE), BF),
            pltpu.VMEM((2, h, 4, n, GROUP), BF),
            pltpu.VMEM((2, h, 16, n, TILE), BF),
            pltpu.VMEM((3, h, 4, n, GROUP), BF),
            pltpu.VMEM((2, h, 2, n, GROUP), BF),
            pltpu.VMEM((1, h, 1, n, GROUP), BF),
            pltpu.VMEM((h, 16, n, TILE), BF),
            pltpu.VMEM((h, 16, n, TILE), BF),
            pltpu.VMEM((h, 8, n, TILE), BF),
            pltpu.VMEM((h, 16, n, TILE), BF),
            pltpu.VMEM((h, 4, n, TILE), BF),
            pltpu.VMEM((h, 4, n, TILE), F32),
            pltpu.VMEM((h, 2, 2, n, GROUP), F32),
            pltpu.VMEM((h, n, TILE), F32),
            pltpu.VMEM((h, n, TILE), F32),
            dma((9,)),
            dma((5, h, 4)),
            dma((5, h, 4)),
            dma((5, h, 4)),
            dma((5, h, 4)),
            dma((10, h)),
            dma((10, h)),
            dma((6, h)),
            dma((6, h, 4)),
            dma((6, h, 4)),
            dma((6, h, 4)),
        ],
        compiler_params=pltpu.CompilerParams(
            collective_id=0, has_side_effects=True, vmem_limit_bytes=62 * 2**20
        ),
        cost_estimate=pl.CostEstimate(flops=9_200_000_000, bytes_accessed=19_000_000, transcendentals=0),
    )(
        leaf_rhs.reshape(TILE, rhs),
        mid_rhs.reshape(TILE, rhs),
        top_rhs.reshape(TILE, rhs),
        leaf_inverse.reshape(GROUP, 8, TILE),
        mid_inverse.reshape(4, TILE, 16, TILE),
        top_inverse.reshape(GROUP, 32, TILE),
        leaf_coupling.reshape(4, 6, TILE, 8, TILE),
        mid_coupling.reshape(2, 4, TILE, 16, TILE),
        leaf_targets[0, 0],
        leaf_counts[0, 0],
        mid_targets[0, 0],
        mid_counts[0, 0],
    )
    return tuple(o.reshape(shape) for o in outs)


def solution(mesh):
    vector = P("leaf", "row", "col", None, None, None)
    inverse = P("leaf", "row", None, None, "col", None, None)
    coupling = P("leaf", "row", None, None, None, "col", None, None)
    placed = (
        vector,
        vector,
        vector,
        inverse,
        inverse,
        inverse,
        coupling,
        coupling,
        P("leaf", "row", None, None),
        P("leaf", "row", None),
        P("leaf", "row", None, None),
        P("leaf", "row", None),
    )
    return jax.shard_map(
        shards, mesh=mesh, in_specs=placed, out_specs=(vector, vector, vector), check_vma=False
    )
```

time: 881 us -> 169 us (0.19)
  waiting for transfers between devices: 715 us -> 0 us
  Pallas kernels: 0 us -> 164 us
  blocking collectives: 49.3 us -> 0 us
  local copies, waits for them, and re-layouts: 48.5 us -> 4.7 us
  matrix products: 42.1 us -> 0 us
  between operations: 14.3 us -> 0.64 us
  other arithmetic: 9.45 us -> 0 us
    reduce_scatter x10 -> x0, waiting for transfers between devices: 490 us -> none  [the longest x5 403 us: group_sum(): lax.psum_scatter(partial_value.astype(jnp.bfloat16), ('leaf', 'row'), sca...]
    all_gather x5 -> x0, waiting for transfers between devices: 224 us -> none  [gather_all(): return lax.all_gather(vector, ('leaf', 'row'), axis=0, tiled=True)]
    pallas_call x0 -> x1, Pallas kernels: none -> 164 us  [shards(): pl.pallas_call(functools.partial(kernel, n), out_shape=(out, out, out), i...]
    all_gather x5 -> x0, blocking collectives: 49.3 us -> none  [row_tiles(): return lax.all_gather(vector, 'col', axis=0, tiled=True)]
    dot_general x12 -> x0, matrix products: 42.1 us -> none  [the longest x2 11.5 us: couple_forward(): jnp.einsum('ksc,kcn->ksn', matrix, inputs, preferred_element_type=jnp.flo...]
    another operation x4 -> x0, local copies, waits for them, and re-layouts: 18.1 us -> none  [the longest x2 17.7 us: couple_backward(): matrix = coupling.reshape(sources, slot_count * tile_rows, -1)]
    convert_element_type x8 -> x0, local copies, waits for them, and re-layouts: 11.8 us -> none  [the longest x3 7.6 us: group_sum(): partial_value.astype(jnp.bfloat16)]
  transfers between devices with their start and end apart: 15 -> 0, of which waited for: 15 -> 0; matrix products, arithmetic and copies ran while one was open for 2% -> 0% of each run, Pallas kernels for 0% -> 0%
where the time goes in v1:
time: 169 us
  Pallas kernels  164 us (97%)
  local copies, waits for them, and re-layouts  4.7 us (3%)
    pallas_call x1, Pallas kernels, shards(): pl.pallas_call(functools.partial(kernel, n), out_shape=(out, out, out), i...  164 us
    unnamed x3, local copies, waits for them, and re-layouts  4.7 us

profile of v1, /device:TPU:1, one launch (start us, length us, event | category | flops | bytes accessed | tf_op | source)
XLA Modules:
  0.0 169.1 jit_solution(1145740357903643167)
XLA Ops:
  0.6 163.8 %shard_map.139 = (f32[128,256]{1,0:T(8,128)}, f32[128,256]{1,0:T(8,128)}, f32[128,256]{1,0:T(8,128)}) custom-call(f32[128,256]{1,0:T(8,128)} %bitcast.23, f32[128,256]{1,0:T(8,128)} %bitcast.24, f32[128,256]{1,0:T(8,128)} %bitcast.25, bf16[512,8,128]{2,1,0:T(8,128)(2,1)} %bitcast.22, bf16[4,128,16,128]{3,2,1,0:T(8,128)(2,1)} %bitcast.21, ...), custom_call_target="tpu_custom_call" | custom-call | flops 9200000000 | bytes 19000000 | tf_op jit(solution)/shard_map/pallas_call | solution.py:441
  164.4 1.6 copy.18
  166.0 1.6 copy.19
  167.6 1.6 copy.20

commit v2 on v1

--- a/solution.py
+++ b/solution.py
@@ -184,7 +184,7 @@
     }
 
     barrier = pltpu.get_barrier_semaphore()
-    reached = [sibling] + [plane(a, b) for a in range(4) for b in range(4) if a or b]
+    reached = [sibling] + [plane(0, k) for k in range(1, 4)] + [plane(k, 0) for k in range(1, 4)]
     reached += [(y, row, cs[k]) for k in range(1, 4)]
     for device in reached:
         pl.semaphore_signal(barrier, inc=1, device_id=device, device_id_type=MESH)
@@ -227,20 +227,18 @@
         def gather_done(ph, x, at, dy):
             arrived(x.at[h, eo, at[dy]], ag_rxs.at[ph, h, dy])
 
-        def products(w, wat, x, at, core, dys):
+        def gathered_product(ph, w, wat, x, at, dys):
+            def part(core, dy):
+                return jnp.dot(w[core, wat[dy]], x[h, core, at[dy]], preferred_element_type=F32)
+
             total = None
             for dy in dys:
-                part = jnp.dot(w[core, wat[dy]], x[h, core, at[dy]], preferred_element_type=F32)
-                total = part if total is None else total + part
-            return total
-
-        def gathered_product(ph, w, wat, x, at, dys):
-            for dy in dys:
                 gather_forward(ph, x, at, dy)
-            total = products(w, wat, x, at, e, dys)
+                total = part(e, dy) if total is None else total + part(e, dy)
             for dy in dys:
                 gather_done(ph, x, at, dy)
-            return total + products(w, wat, x, at, eo, dys)
+                total = total + part(eo, dy)
+            return total
 
         def column_send(ph, total):
             for q in range(4):
@@ -328,7 +326,12 @@
         column_send(2, gathered_product(2, wm, pars, x3, pars, (0, 1)))
         for dy in (3, 2):
             gather_done(1, x2, ys, dy)
-        top_part[h] = products(gt, ys, x2, ys, e, far) + products(gt, ys, x2, ys, eo, far)
+        total = None
+        for core in (e, eo):
+            for dy in far:
+                part = jnp.dot(gt[core, ys[dy]], x2[h, core, ys[dy]], preferred_element_type=F32)
+                total = part if total is None else total + part
+        top_part[h] = total
         yield
         drain()
         forward = column_sum(2)
@@ -401,16 +404,19 @@
         drain()
 
     running = [chain(h) for h in range(CHAINS)]
-    step = 0
-    while running:
-        alive = []
+    order = ((0,), (1, 2), (3, 4), (5, 6), (7, 8), (9, 10), (11,), (12, 13), (14, 15), (16, 17), (18,), (19,), (20,))
+    for turn in order:
         for g in running:
-            if next(g, "end") != "end":
-                alive.append(g)
-        running = alive
-        for task in tasks.get(step, ()):
-            task()
-        step += 1
+            for step in turn:
+                next(g, None)
+        for step in turn:
+            for task in tasks.get(step, ()):
+                task()
+
+
+def write_out(*refs):
+    for k in range(3):
+        refs[3 + k][...] = refs[k][...]
 
 
 def shards(
@@ -501,6 +507,12 @@
         mid_targets[0, 0],
         mid_counts[0, 0],
     )
+    outs = pl.pallas_call(
+        write_out,
+        out_shape=(out, out, out),
+        in_specs=[vmem] * 3,
+        out_specs=(vmem, vmem, vmem),
+    )(*outs)
     return tuple(o.reshape(shape) for o in outs)
 
 

time: 169 us -> 156 us (0.923)
  Pallas kernels: 164 us -> 155 us
  local copies, waits for them, and re-layouts: 4.7 us -> 0 us
    pallas_call x1, Pallas kernels: 164 us -> 154 us  [shards(): pl.pallas_call(functools.partial(kernel, n), out_shape=(out, out, out), i...]
    unnamed x3 -> x0, local copies, waits for them, and re-layouts: 4.7 us -> none
    pallas_call x0 -> x1, Pallas kernels: none -> 1.78 us  [shards(): pl.pallas_call(write_out, out_shape=(out, out, out), in_specs=[vmem] * 3,...]
where the time goes in v2:
time: 156 us
  Pallas kernels  155 us (99%)
    pallas_call x1, Pallas kernels, shards(): pl.pallas_call(functools.partial(kernel, n), out_shape=(out, out, out), i...  154 us

profile of v2, /device:TPU:1, one launch (start us, length us, event | category | flops | bytes accessed | tf_op | source)
XLA Modules:
  0.0 156.0 jit_solution(1937752891694374558)
XLA Ops:
  0.6 153.6 %shard_map.139 = (f32[128,256]{1,0:T(8,128)}, f32[128,256]{1,0:T(8,128)}, f32[128,256]{1,0:T(8,128)}) custom-call(f32[128,256]{1,0:T(8,128)} %bitcast.20, f32[128,256]{1,0:T(8,128)} %bitcast.21, f32[128,256]{1,0:T(8,128)} %bitcast.22, bf16[512,8,128]{2,1,0:T(8,128)(2,1)} %bitcast.19, bf16[4,128,16,128]{3,2,1,0:T(8,128)(2,1)} %bitcast.18, ...), custom_call_target="tpu_custom_call" | custom-call | flops 9200000000 | bytes 19000000 | tf_op jit(solution)/shard_map/pallas_call | solution.py:447
  154.2 1.8 %shard_map.140 = (f32[128,256]{1,0:T(8,128)}, f32[128,256]{1,0:T(8,128)}, f32[128,256]{1,0:T(8,128)}) custom-call(f32[128,256]{1,0:T(8,128)} %get-tuple-element.9.refs_0_, f32[128,256]{1,0:T(8,128)} %get-tuple-element.10.refs_1_, f32[128,256]{1,0:T(8,128)} %get-tuple-element.11.refs_2_), custom_call_target="tpu_custom_call" | custom-call | tf_op jit(solution)/shard_map/pallas_call | solution.py:510

commit v3 on v2

--- a/solution.py
+++ b/solution.py
@@ -94,6 +94,7 @@
 
     ys, zs, cs = partners(y), partners(z), partners(c)
     pars = [par, 1 - par]
+    hops = (0, 1, 2, 1)
     sibling = (y, z * 2 + eo, c)
 
     def plane(dy, dz):
@@ -207,13 +208,16 @@
         def arrived(ref, sem):
             remote(ref, ref, sem, sem, sibling).wait_recv()
 
-        def gather_send(ph, x, at, value, dys):
+        def gather_send(ph, x, at, value, dys, later=()):
             mine = x.at[h, e, at[0], pl.ds(z * TILE, TILE)]
             x[h, e, at[0], pl.ds(z * TILE, TILE), :] = value
-            for dy in dys:
-                for dz in (2, 1, 3, 0):
-                    if dy or dz:
-                        remote(mine, mine, ag_tx.at[ph, h, dy], ag_rx.at[ph, h, dy], plane(dy, dz)).start()
+            far_first = sorted(
+                ((dy, dz) for dy in dys for dz in range(4) if dy or dz), key=lambda p: -hops[p[0]] - hops[p[1]]
+            )
+            far_first += [(dy, dz) for dy in later for dz in (2, 1, 3, 0)]
+            for dy, dz in far_first:
+                remote(mine, mine, ag_tx.at[ph, h, dy], ag_rx.at[ph, h, dy], plane(dy, dz)).start()
+            for dy in (*dys, *later):
                 tiles = 4 if dy else 3
                 sent.append((x.at[h, 0, 0, pl.ds(0, tiles * TILE)], ag_tx.at[ph, h, dy]))
 
@@ -232,9 +236,13 @@
                 return jnp.dot(w[core, wat[dy]], x[h, core, at[dy]], preferred_element_type=F32)
 
             total = None
-            for dy in dys:
+            for k, dy in enumerate(dys):
+                if k == 1:
+                    yield
                 gather_forward(ph, x, at, dy)
                 total = part(e, dy) if total is None else total + part(e, dy)
+            if len(dys) == 1:
+                yield
             for dy in dys:
                 gather_done(ph, x, at, dy)
                 total = total + part(eo, dy)
@@ -309,21 +317,24 @@
 
         gather_send(0, x1, zero, leaf_rhs[:, cols].astype(BF), (0,))
         yield
-        column_send(0, gathered_product(0, wl, zero, x1, zero, (0,)))
+        total = yield from gathered_product(0, wl, zero, x1, zero, (0,))
+        column_send(0, total)
         yield
         drain()
         forward = column_sum(0)
-        gather_send(1, x2, ys, forward.astype(BF), (1, 0, 2, 3))
+        gather_send(1, x2, ys, forward.astype(BF), (1, 0), (2, 3))
         lf[h] = forward.T
         yield
-        column_send(1, gathered_product(1, gm, pars, x2, ys, (0, 1)))
+        total = yield from gathered_product(1, gm, pars, x2, ys, (0, 1))
+        column_send(1, total)
         yield
         drain()
         gather_send(2, x3, pars, (mid_rhs[:, cols] - column_sum(1)).astype(BF), (1, 0))
         for dy in (3, 2):
             gather_forward(1, x2, ys, dy)
         yield
-        column_send(2, gathered_product(2, wm, pars, x3, pars, (0, 1)))
+        total = yield from gathered_product(2, wm, pars, x3, pars, (0, 1))
+        column_send(2, total)
         for dy in (3, 2):
             gather_done(1, x2, ys, dy)
         total = None
@@ -338,12 +349,14 @@
         gather_send(3, x4, ys, forward.astype(BF), far)
         mf[h] = forward.T
         yield
-        column_send(3, gathered_product(3, hm, ys, x4, ys, (0, 1, 3, 2)) + top_part[h])
+        total = yield from gathered_product(3, hm, ys, x4, ys, (0, 1, 3, 2))
+        column_send(3, total + top_part[h])
         yield
         drain()
         gather_send(4, x5, ys, (top_rhs[:, cols] - column_sum(3)).astype(BF), far)
         yield
-        column_send(4, gathered_product(4, wt, ys, x5, ys, (0, 1, 3, 2)))
+        total = yield from gathered_product(4, wt, ys, x5, ys, (0, 1, 3, 2))
+        column_send(4, total)
         yield
         drain()
         row_send(0, column_sum(4).T.astype(BF))
@@ -404,14 +417,12 @@
         drain()
 
     running = [chain(h) for h in range(CHAINS)]
-    order = ((0,), (1, 2), (3, 4), (5, 6), (7, 8), (9, 10), (11,), (12, 13), (14, 15), (16, 17), (18,), (19,), (20,))
-    for turn in order:
-        for g in running:
-            for step in turn:
-                next(g, None)
-        for step in turn:
-            for task in tasks.get(step, ()):
+    for what in "ab0aaba1bab2aba3bab4aba5babababababababbaabbaabbaabbababab":
+        if what.isdigit():
+            for task in tasks[int(what)]:
                 task()
+        else:
+            next(running["ab".index(what)], None)
 
 
 def write_out(*refs):

time: 156 us -> 152 us (0.974)
  Pallas kernels: 155 us -> 151 us
    pallas_call x1, Pallas kernels: 154 us -> 150 us  [shards(): pl.pallas_call(functools.partial(kernel, n), out_shape=(out, out, out), i...]
where the time goes in v3:
time: 152 us
  Pallas kernels  151 us (99%)
    pallas_call x1, Pallas kernels, shards(): pl.pallas_call(functools.partial(kernel, n), out_shape=(out, out, out), i...  150 us

profile of v3, /device:TPU:1, one launch (start us, length us, event | category | flops | bytes accessed | tf_op | source)
XLA Modules:
  0.0 152.1 jit_solution(10030343999885312774)
XLA Ops:
  0.6 149.7 %shard_map.139 = (f32[128,256]{1,0:T(8,128)}, f32[128,256]{1,0:T(8,128)}, f32[128,256]{1,0:T(8,128)}) custom-call(f32[128,256]{1,0:T(8,128)} %bitcast.20, f32[128,256]{1,0:T(8,128)} %bitcast.21, f32[128,256]{1,0:T(8,128)} %bitcast.22, bf16[512,8,128]{2,1,0:T(8,128)(2,1)} %bitcast.19, bf16[4,128,16,128]{3,2,1,0:T(8,128)(2,1)} %bitcast.18, ...), custom_call_target="tpu_custom_call" | custom-call | flops 9200000000 | bytes 19000000 | tf_op jit(solution)/shard_map/pallas_call | solution.py:458
  150.3 1.8 %shard_map.140 = (f32[128,256]{1,0:T(8,128)}, f32[128,256]{1,0:T(8,128)}, f32[128,256]{1,0:T(8,128)}) custom-call(f32[128,256]{1,0:T(8,128)} %get-tuple-element.9.refs_0_, f32[128,256]{1,0:T(8,128)} %get-tuple-element.10.refs_1_, f32[128,256]{1,0:T(8,128)} %get-tuple-element.11.refs_2_), custom_call_target="tpu_custom_call" | custom-call | tf_op jit(solution)/shard_map/pallas_call | solution.py:521
